TPU v7x, 32 devices: a whole 2x2x4 slice. The times are simulated.
32 devices in a mesh: groups: 2 (over y), ops: 16 (over z, x, core).
Axes of the slice: x: 2, y: 2, z: 4, core: 2. Of those that a mesh axis runs over, the one named last changes fastest.
Arguments:
- psi_start: float32 [1024, 128], P(('groups', 'ops')), parts along dimension 0, may hold values from -6 to 6
- precond: float32 [1024, 128], P(('groups', 'ops')), parts along dimension 0, may hold values from 0.02 to 0.2
- left_ops: bfloat16 [512, 64, 64], P(('groups', 'ops')), parts along dimension 0, may hold values from -0.1875 to 0.1875
- right_ops: bfloat16 [512, 128, 128], P(('groups', 'ops')), parts along dimension 0, may hold values from -0.5 to 0.5
- term_in: int32 [512, 16], P(('groups', 'ops')), parts along dimension 0, may hold values from 0 to 7
- term_out: int32 [512, 16], P(('groups', 'ops')), parts along dimension 0, may hold values from 0 to 7
- term_live: int32 [32], P(('groups', 'ops')), parts along dimension 0, may hold values from 1 to 16, as said below
- left_rot: float32 [1024, 64], P(('groups', 'ops')), parts along dimension 0, may hold values from -0.75 to 0.75
Outputs:
- start_energy: float32 [2], P('groups'), parts along dimension 0
- energies: float32 [6], P('groups'), parts along dimension 0
- shifted: float32 [1024, 128], P(('groups', 'ops')), parts along dimension 0
There are 2 independent parts, one for each index of `groups`. A program takes and returns all parts, laid end to end along the dimension named above; each array names one. Nothing has to cross between parts.
Inputs may be any that keep to these rules, and one draw needn't show every extreme that they name: `term_live`: some index of ops has all 16 slots live in every draw.
All inputs are finite; a program needn't handle non-finite values.
Results may differ from a plain program's by a relative error of at most 0.011.
Values may be sent and summed in bfloat16 or wider, within the bound.
A program may use at most 64 MiB of HBM per device.

v0:
```python
import jax
import jax.numpy as jnp
from jax import lax
from jax.sharding import PartitionSpec as P

ITERS = 4


def from_partner(block, axis, stride):
    count = lax.axis_size(axis)
    route = []
    for low in range(count):
        high = low | 1 << stride
        if high != low and high < count:
            route += [(low, high), (high, low)]
    return lax.ppermute(block, axis, route)


def local_terms(whole_b, left_ops, right_ops, term_in, term_out, live_count):
    block_rows = left_ops.shape[1]
    width = whole_b.shape[1]
    sector_count = whole_b.shape[0] // block_rows
    slot_count = left_ops.shape[0]
    pair_count = term_in.shape[1]
    blocks = whole_b.reshape(sector_count, block_rows, width)
    chosen = blocks[term_in]
    inner = jnp.einsum(
        "tab,tpbc->tpac", left_ops, chosen, preferred_element_type=jnp.float32
    ).astype(jnp.bfloat16)
    image = jnp.einsum("tpac,tdc->tpad", inner, right_ops, preferred_element_type=jnp.float32)
    alive = jnp.arange(slot_count, dtype=jnp.int32) < live_count
    onehot = (
        term_out[:, :, None] == jnp.arange(sector_count, dtype=jnp.int32)[None, None, :]
    ) & alive[:, None, None]
    onehot = onehot.astype(jnp.float32).reshape(slot_count * pair_count, sector_count)
    flat = image.reshape(slot_count * pair_count, block_rows * width)
    total = jnp.dot(
        onehot.T, flat, precision=lax.Precision.HIGHEST, preferred_element_type=jnp.float32
    )
    return total.reshape(whole_b.shape[0], width)


def body(psi_start, precond, left_ops, right_ops, term_in, term_out, term_live, left_rot):
    live_count = term_live[0]
    own_rows = psi_start.shape[0]
    offset = lax.axis_index("ops") * own_rows
    found = []
    vector, scaling = (
        lax.all_gather(psi_start, "ops", axis=0, tiled=True),
        lax.all_gather(precond, "ops", axis=0, tiled=True),
    )
    for step_index in range(ITERS):
        terms = local_terms(
            vector.astype(jnp.bfloat16), left_ops, right_ops, term_in, term_out, live_count
        )
        image = lax.psum(terms, "ops")
        quotient = jnp.sum(vector * image) / jnp.sum(vector * vector)
        found.append(quotient)
        update = vector - scaling * (image - quotient * vector)
        vector = update / jnp.sqrt(jnp.mean(update * update) + 1e-06)
    mine = lax.dynamic_slice_in_dim(vector, offset, own_rows, 0)
    partial_value = jnp.dot(
        left_rot.T, mine, precision=lax.Precision.HIGHEST, preferred_element_type=jnp.float32
    )
    half = partial_value.shape[0] // 2
    parity = lax.axis_index("ops") % 2
    keep_part = lax.dynamic_slice_in_dim(partial_value, parity * half, half, 0)
    give_part = lax.dynamic_slice_in_dim(partial_value, (1 - parity) * half, half, 0)
    received = from_partner(give_part, "ops", 0)
    first = jnp.stack(found[:1])
    later = jnp.stack(found[1:])
    return (first, later, keep_part + received)


def solution(mesh):
    return jax.shard_map(
        body,
        mesh=mesh,
        in_specs=(
            P(("groups", "ops"), None),
            P(("groups", "ops"), None),
            P(("groups", "ops"), None, None),
            P(("groups", "ops"), None, None),
            P(("groups", "ops"), None),
            P(("groups", "ops"), None),
            P(("groups", "ops")),
            P(("groups", "ops"), None),
        ),
        out_specs=(P("groups"), P("groups"), P(("groups", "ops"), None)),
        check_vma=False,
    )
```

profile of v0, /device:TPU:0, one launch (start us, length us, event | category | flops | bytes accessed | tf_op | source)
XLA Modules:
  0.0 508.7 jit_solution(10865390592869691232)
XLA Ops:
  8.1 24.0 %all_gather.6 = f32[512,128]{1,0:T(8,128)S(1)} all-gather(f32[32,128]{1,0:T(8,128)} %param.8), channel_id=1, replica_groups=mesh['groups'=2,'ops'=16] {'ops'}, dimensions={0}, use_global_device_ids=true | all-gather | bytes 278528 | tf_op jit(solution)/shard_map/all_gather | solution.py:49
  33.7 3.1 gather_fusion
  36.8 7.8 %fusion.18 = f32[16,16,64,128]{3,2,1,0:T(8,128)} fusion(bf16[16,16,64,128]{3,2,1,0:T(8,128)(2,1)} %bitcast.90, bf16[16,128,128]{2,1,0:T(8,128)(2,1)S(1)} %copy-done, bf16[16,64,64]{2,1,0:T(8,128)(2,1)S(1)} %copy-done.1), kind=kOutput, calls=%fused_computation.22 | convolution fusion | flops 807403520 | bytes 13238272 | tf_op jit(solution)/shard_map/tpac,tdc->tpad/dot_general | solution.py:30
  44.6 10.5 %fusion.9 = f32[8,8192]{1,0:T(8,128)S(1)} fusion(f32[32,8,64,128]{3,2,1,0:T(8,128)} %bitcast.86, s32[256]{0:T(256)S(1)} %eq.10, pred[256]{0:T(512)(128)(4,1)S(1)} %and.15), kind=kOutput, calls=%fused_computation.13 | convolution fusion | flops 201330688 | bytes 8652032 | tf_op jit(solution)/shard_map/dot_general | solution.py:37
  55.9 18.4 %all_gather.7 = f32[512,128]{1,0:T(8,128)S(1)} all-gather(f32[32,128]{1,0:T(8,128)S(1)} %copy-done.2), channel_id=1, replica_groups=mesh['groups'=2,'ops'=16] {'ops'}, dimensions={0}, use_global_device_ids=true | all-gather | bytes 278528 | tf_op jit(solution)/shard_map/all_gather | solution.py:50
  74.3 68.0 %all-reduce.5.cloned.1.call-done = f32[512,128]{1,0:T(8,128)} async-done(((f32[512,128]{1,0:T(8,128)}), f32[512,128]{1,0:T(8,128)}) %all-reduce.5.cloned.1.call-update) | async-done | bytes 262160 | tf_op jit(solution)/shard_map/psum | solution.py:56
  147.6 3.1 gather_fusion.1
  150.6 7.8 %fusion.16 = f32[16,16,64,128]{3,2,1,0:T(8,128)} fusion(bf16[16,16,64,128]{3,2,1,0:T(8,128)(2,1)} %bitcast.91, bf16[16,128,128]{2,1,0:T(8,128)(2,1)S(1)} %copy-done, bf16[16,64,64]{2,1,0:T(8,128)(2,1)S(1)} %copy-done.1), kind=kOutput, calls=%fused_computation.20 | convolution fusion | flops 807403520 | bytes 13238272 | tf_op jit(solution)/shard_map/tpac,tdc->tpad/dot_general | solution.py:30
  158.4 10.5 %fusion.6 = f32[8,8192]{1,0:T(8,128)S(1)} fusion(f32[32,8,64,128]{3,2,1,0:T(8,128)} %bitcast.87, s32[256]{0:T(256)S(1)} %eq.10, pred[256]{0:T(512)(128)(4,1)S(1)} %and.15), kind=kOutput, calls=%fused_computation.10 | convolution fusion | flops 201330688 | bytes 8652032 | tf_op jit(solution)/shard_map/dot_general | solution.py:37
  169.9 89.2 %all-reduce.7.cloned.1.call-done = f32[512,128]{1,0:T(8,128)} async-done(((f32[512,128]{1,0:T(8,128)}), f32[512,128]{1,0:T(8,128)}) %all-reduce.7.cloned.1.call-update) | async-done | bytes 262160 | tf_op jit(solution)/shard_map/psum | solution.py:56
  259.2 1.6 multiply_reduce_fusion.7
  262.1 1.6 multiply_reduce_fusion.6
  264.5 3.1 gather_fusion.2
  267.6 7.8 %fusion.14 = f32[16,16,64,128]{3,2,1,0:T(8,128)} fusion(bf16[16,16,64,128]{3,2,1,0:T(8,128)(2,1)} %bitcast.92, bf16[16,128,128]{2,1,0:T(8,128)(2,1)S(1)} %copy-done, bf16[16,64,64]{2,1,0:T(8,128)(2,1)S(1)} %copy-done.1), kind=kOutput, calls=%fused_computation.18 | convolution fusion | flops 807403520 | bytes 13238272 | tf_op jit(solution)/shard_map/tpac,tdc->tpad/dot_general | solution.py:30
  275.3 10.5 %fusion.3 = f32[8,8192]{1,0:T(8,128)S(1)} fusion(f32[32,8,64,128]{3,2,1,0:T(8,128)} %bitcast.88, s32[256]{0:T(256)S(1)} %eq.10, pred[256]{0:T(512)(128)(4,1)S(1)} %and.15), kind=kOutput, calls=%fused_computation.7 | convolution fusion | flops 201330688 | bytes 8652032 | tf_op jit(solution)/shard_map/dot_general | solution.py:37
  286.9 89.2 %all-reduce.9.cloned.1.call-done = f32[512,128]{1,0:T(8,128)} async-done(((f32[512,128]{1,0:T(8,128)}), f32[512,128]{1,0:T(8,128)}) %all-reduce.9.cloned.1.call-update) | async-done | bytes 262160 | tf_op jit(solution)/shard_map/psum | solution.py:56
  376.1 1.7 multiply_reduce_fusion.4
  379.1 1.6 multiply_reduce_fusion.3
  381.4 3.1 gather_fusion.3
  384.5 7.8 %fusion.12 = f32[16,16,64,128]{3,2,1,0:T(8,128)} fusion(bf16[16,16,64,128]{3,2,1,0:T(8,128)(2,1)} %bitcast.89, bf16[16,128,128]{2,1,0:T(8,128)(2,1)S(1)} %copy-done, bf16[16,64,64]{2,1,0:T(8,128)(2,1)S(1)} %copy-done.1), kind=kOutput, calls=%fused_computation.16 | convolution fusion | flops 807403520 | bytes 13238272 | tf_op jit(solution)/shard_map/tpac,tdc->tpad/dot_general | solution.py:30
  392.3 10.5 %fusion = f32[8,8192]{1,0:T(8,128)S(1)} fusion(f32[32,8,64,128]{3,2,1,0:T(8,128)} %bitcast.85, s32[256]{0:T(256)S(1)} %eq.10, pred[256]{0:T(512)(128)(4,1)S(1)} %and.15), kind=kOutput, calls=%fused_computation.4 | convolution fusion | flops 201330688 | bytes 8652032 | tf_op jit(solution)/shard_map/dot_general | solution.py:37
  403.6 89.4 %all-reduce.11.cloned.1.call-done = f32[512,128]{1,0:T(8,128)} async-done(((f32[512,128]{1,0:T(8,128)}), f32[512,128]{1,0:T(8,128)}) %all-reduce.11.cloned.1.call-update) | async-done | bytes 262160 | tf_op jit(solution)/shard_map/psum | solution.py:56
  493.0 1.7 multiply_reduce_fusion.1
  496.0 1.6 multiply_reduce_fusion
  (39 shorter events, 11.2 us)
Async XLA Ops:
  7.2 29.6 %copy-start = (bf16[16,128,128]{2,1,0:T(8,128)(2,1)S(1)}, bf16[16,128,128]{2,1,0:T(8,128)(2,1)}, u32[]{:S(2)}) copy-start(bf16[16,128,128]{2,1,0:T(8,128)(2,1)} %param.11) | copy-start | bytes 1572868
  7.2 135.1 %all-reduce.5.cloned.1.call-start = ((), (), s32[]{:S(2)}) async-start(), calls=%async_computation | async-start | bytes 524288 | tf_op jit(solution)/shard_map/psum | solution.py:56
  33.7 3.1 copy-start.1
  44.6 11.3 %copy-start.2 = (f32[32,128]{1,0:T(8,128)S(1)}, f32[32,128]{1,0:T(8,128)}, u32[]{:S(2)}) copy-start(f32[32,128]{1,0:T(8,128)} %param.9) | copy-start | bytes 49156
  55.8 203.3 %all-reduce.7.cloned.1.call-start = ((), (), s32[]{:S(2)}) async-start(), calls=%async_computation.1 | async-start | bytes 524288 | tf_op jit(solution)/shard_map/psum | solution.py:56
  169.7 206.4 %all-reduce.9.cloned.1.call-start = ((), (), s32[]{:S(2)}) async-start(), calls=%async_computation.2 | async-start | bytes 524288 | tf_op jit(solution)/shard_map/psum | solution.py:56
  286.6 206.4 %all-reduce.11.cloned.1.call-start = ((), (), s32[]{:S(2)}) async-start(), calls=%async_computation.3 | async-start | bytes 524288 | tf_op jit(solution)/shard_map/psum | solution.py:56
  392.3 106.0 %copy-start.3 = (f32[32,64]{1,0:T(8,128)S(1)}, f32[32,64]{1,0:T(8,128)}, u32[]{:S(2)}) copy-start(f32[32,64]{1,0:T(8,128)} %param.15) | copy-start | bytes 24580
  498.6 1.4 collective-permute-start
Sparse Core Ops, SparseCore 0:
  56.0 86.2 all-reduce.4
  169.8 89.3 all-reduce.6
  286.7 89.2 all-reduce.8
  403.7 89.2 all-reduce.10
where the time goes:
time: 517 us; the launch traced here: 509 us
  waiting for transfers between devices  336 us (65%)
  matrix products  73.3 us (14%)
  blocking collectives  42.4 us (8%)
  between operations  24.2 us (5%)
  local copies, waits for them, and re-layouts  16.3 us (3%)
  other arithmetic  15.2 us (3%)
    psum x4, waiting for transfers between devices, body(): image = lax.psum(terms, 'ops')  336 us
    dot_general x4, matrix products, local_terms(): jnp.dot(onehot.T, flat, precision=lax.Precision.HIGHEST, preferred_elemen...  41.9 us
    dot_general x4, matrix products, local_terms(): jnp.einsum('tpac,tdc->tpad', inner, right_ops, preferred_element_type=jnp...  31.1 us
    all_gather x1, blocking collectives, body(): lax.all_gather(psi_start, 'ops', axis=0, tiled=True)  24 us
    all_gather x1, blocking collectives, body(): lax.all_gather(precond, 'ops', axis=0, tiled=True)  18.4 us
    gather x4, local copies, waits for them, and re-layouts, local_terms(): chosen = blocks[term_in]  12.3 us
  transfers between devices with their start and end apart: 5, of which 5 were waited for; matrix products, arithmetic and copies ran while one was open for 0% of the time, Pallas kernels for 0%

commit v1 on v0

v1 whole, which is shorter than its diff:
```python
import functools
import jax
import jax.numpy as jnp
from jax import lax
from jax.experimental import pallas as pl
from jax.experimental.pallas import tpu as pltpu
from jax.sharding import PartitionSpec as P

ITERS = 4
SUB = 16
F32 = jnp.float32
BF16 = jnp.bfloat16


def from_partner(block, axis, stride):
    count = lax.axis_size(axis)
    route = []
    for low in range(count):
        high = low | 1 << stride
        if high != low and high < count:
            route += [(low, high), (high, low)]
    return lax.ppermute(block, axis, route)


def local_terms(whole_b, left_ops, right_ops, term_in, term_out, live_count):
    block_rows = left_ops.shape[1]
    width = whole_b.shape[1]
    sector_count = whole_b.shape[0] // block_rows
    slot_count = left_ops.shape[0]
    pair_count = term_in.shape[1]
    blocks = whole_b.reshape(sector_count, block_rows, width)
    chosen = blocks[term_in]
    inner = jnp.einsum(
        "tab,tpbc->tpac", left_ops, chosen, preferred_element_type=F32
    ).astype(BF16)
    image = jnp.einsum("tpac,tdc->tpad", inner, right_ops, preferred_element_type=F32)
    alive = jnp.arange(slot_count, dtype=jnp.int32) < live_count
    onehot = (
        term_out[:, :, None] == jnp.arange(sector_count, dtype=jnp.int32)[None, None, :]
    ) & alive[:, None, None]
    onehot = onehot.astype(F32).reshape(slot_count * pair_count, sector_count)
    flat = image.reshape(slot_count * pair_count, block_rows * width)
    total = jnp.dot(
        onehot.T, flat, precision=lax.Precision.HIGHEST, preferred_element_type=F32
    )
    return total.reshape(whole_b.shape[0], width)


def pair_body(psi_start, precond, left_ops, right_ops, term_in, term_out, term_live, left_rot):
    live_count = term_live[0]
    own_rows = psi_start.shape[0]
    offset = lax.axis_index("ops") * own_rows
    found = []
    vector, scaling = (
        lax.all_gather(psi_start, "ops", axis=0, tiled=True),
        lax.all_gather(precond, "ops", axis=0, tiled=True),
    )
    for step_index in range(ITERS):
        terms = local_terms(
            vector.astype(BF16), left_ops, right_ops, term_in, term_out, live_count
        )
        image = lax.psum(terms, "ops")
        quotient = jnp.sum(vector * image) / jnp.sum(vector * vector)
        found.append(quotient)
        update = vector - scaling * (image - quotient * vector)
        vector = update / jnp.sqrt(jnp.mean(update * update) + 1e-06)
    mine = lax.dynamic_slice_in_dim(vector, offset, own_rows, 0)
    partial_value = jnp.dot(
        left_rot.T, mine, precision=lax.Precision.HIGHEST, preferred_element_type=F32
    )
    half = partial_value.shape[0] // 2
    parity = lax.axis_index("ops") % 2
    keep_part = lax.dynamic_slice_in_dim(partial_value, parity * half, half, 0)
    give_part = lax.dynamic_slice_in_dim(partial_value, (1 - parity) * half, half, 0)
    received = from_partner(give_part, "ops", 0)
    return (jnp.stack(found[:1]), jnp.stack(found[1:]), keep_part + received)


def iota(shape, dim):
    return lax.broadcasted_iota(jnp.int32, shape, dim)


def kernel(
    n,
    live_ref, psi_ref, pre_ref, left_ref, right_ref, tin_ref, tout_ref, rot_ref,
    first_ref, later_ref, out_ref,
    counts, inner, image, xsend, xbuf, rsend, rbuf, qsend, qbuf, usend, ubuf, part, got,
    x_out, x_in, r_out, r_in, q_out, q_in, u_out, u_in, p_out, p_in,
):
    me = lax.axis_index("ops")
    slots, bl = left_ref.shape[0], left_ref.shape[1]
    br = right_ref.shape[1]
    pairs = tin_ref.shape[1]
    own = psi_ref.shape[0]
    per = bl // own
    sectors = n // per
    deep = bl // SUB
    st = sectors * SUB
    entries = n * own * br

    barrier = pltpu.get_barrier_semaphore()

    def greet(k, carry):
        pl.semaphore_signal(barrier, inc=1, device_id={"ops": lax.rem(me + k, n)},
                            device_id_type=pl.DeviceIdType.MESH)
        return carry

    lax.fori_loop(1, n, greet, 0)

    def copy(src, dst, out_sem, in_sem, to):
        return pltpu.make_async_remote_copy(
            src_ref=src, dst_ref=dst, send_sem=out_sem, recv_sem=in_sem,
            device_id={"ops": to}, device_id_type=pl.DeviceIdType.MESH)

    def x_copy(i, to, slot):
        return copy(xsend.at[i], xbuf.at[i, slot], x_out.at[i, to], x_in.at[i, slot], to)

    def u_copy(i, to, slot):
        return copy(usend.at[i], ubuf.at[i, slot], u_out.at[i, to], u_in.at[i, slot], to)

    def r_copy(i, to, slot):
        return copy(rsend.at[i, to], rbuf.at[i, slot], r_out.at[i, to], r_in.at[i, slot], to)

    def q_copy(i, to, slot):
        return copy(qsend.at[i], qbuf.at[i, slot], q_out.at[i, to], q_in.at[i, slot], to)

    def each(act):
        def one(k, carry):
            act(lax.rem(me + k, n))
            return carry
        lax.fori_loop(1, n, one, 0)

    def start(makers, i):
        def act(to):
            for make in makers:
                make(i, to, me).start()
        each(act)

    def arrive(makers, i):
        def act(frm):
            for make in makers:
                make(i, frm, frm).wait_recv()
        each(act)

    def sent(makers, i):
        def act(to):
            for make in makers:
                make(i, to, me).wait_send()
        each(act)

    def offer(i, u, extra):
        rows = jnp.concatenate([jnp.sum(u * u, axis=0, keepdims=True), extra], axis=0)
        usend[i] = rows
        ubuf[i, me] = rows

    def offer_x(i, ub):
        xsend[i] = ub
        xbuf[i, me] = ub

    def build_counts():
        live = live_ref[0]
        flat = slots * pairs
        row, col = iota((flat, slots), 0), iota((flat, slots), 1)
        spread = (row // pairs == col).astype(BF16)
        prow, pcol = iota((flat, pairs), 0), iota((flat, pairs), 1)
        ins = jnp.dot(spread, tin_ref[...].astype(F32).astype(BF16), preferred_element_type=F32)
        ins = jnp.sum(jnp.where(prow % pairs == pcol, ins, 0.0), axis=1, keepdims=True)
        outs = lax.dot_general(tout_ref[...].astype(F32).astype(BF16), spread,
                               (((0,), (1,)), ((), ())), preferred_element_type=F32)
        orow, ocol = iota((pairs, flat), 0), iota((pairs, flat), 1)
        outs = jnp.sum(jnp.where(ocol % pairs == orow, outs, 0.0), axis=0, keepdims=True)
        target = (iota((st, flat), 0) // SUB).astype(F32)
        goes = (outs == target).astype(F32).astype(BF16)
        slot = iota((flat, st), 0) // pairs
        sector = (iota((flat, st), 1) // SUB).astype(F32)
        comes = jnp.where(ins == sector, 1.0, 0.0)
        comes = jnp.where(slot < live, comes, 0.0)
        same = (iota((st, st), 0) % SUB == iota((st, st), 1) % SUB).astype(F32)
        for j in range(slots):
            these = jnp.where(slot == j, comes, 0.0).astype(BF16)
            c = jnp.dot(goes, these, preferred_element_type=F32) * same
            c = c.astype(BF16)
            counts[:, 2 * j * st:(2 * j + 1) * st] = c
            counts[:, (2 * j + 1) * st:(2 * j + 2) * st] = c

    def apply(i):
        blocks = [xbuf[i, t * per:(t + 1) * per].reshape(bl, br) for t in range(sectors)]
        x = jnp.concatenate(blocks, axis=1)
        inner[...] = jnp.dot(left_ref[...].reshape(slots * bl, bl), x,
                             preferred_element_type=F32).astype(BF16)
        for j in range(slots):
            y = jnp.concatenate(
                [inner[j * bl:(j + 1) * bl, s * br:(s + 1) * br] for s in range(sectors)], axis=0)
            z = lax.dot_general(y, right_ref[j], (((1,), (1,)), ((), ())),
                                preferred_element_type=F32)
            hi = z.astype(BF16)
            lo = (z - hi.astype(F32)).astype(BF16)
            for which, value in enumerate((hi, lo)):
                top = (2 * j + which) * st
                for a in range(deep):
                    image[top:top + st, a * br:(a + 1) * br] = jnp.concatenate(
                        [value[s * bl + a * SUB:s * bl + (a + 1) * SUB] for s in range(sectors)],
                        axis=0)
        return jnp.dot(counts[...], image[...], preferred_element_type=F32)

    v = psi_ref[...]
    ub = v.astype(BF16)
    offer_x(0, ub)
    offer(0, v, jnp.zeros((1, br), F32))
    pl.semaphore_wait(barrier, n - 1)
    start((x_copy, u_copy), 0)
    build_counts()
    pre = pre_ref[...]
    scale = jnp.ones((1, 1), F32)
    u = v
    overlap = jnp.zeros((1, 1), F32)
    square = overlap

    def total(rows):
        return jnp.sum(rows, axis=1, keepdims=True)

    for i in range(ITERS + 1):
        if i < ITERS:
            arrive((x_copy, u_copy), i)
        else:
            arrive((u_copy,), i)
        rows = jnp.sum(ubuf[i], axis=0)
        usq = total(rows[0:1])
        if i > 0:
            quotient = (overlap + total(rows[1:2])) / square
            if i == 1:
                first_ref[0] = jnp.sum(quotient)
            else:
                later_ref[i - 2] = jnp.sum(quotient)
            scale = lax.rsqrt(usq * (1.0 / entries) + 1e-06)
        if i == ITERS:
            break
        v = u * scale
        square = usq * scale * scale
        acc = apply(i)
        dots = jnp.zeros((own, br), F32)
        for o in range(n):
            t, h = o // per, o % per
            steps = own // SUB
            piece = jnp.concatenate(
                [acc[t * SUB:(t + 1) * SUB, (h * steps + a) * br:(h * steps + a + 1) * br]
                 for a in range(steps)], axis=0)
            rsend[i, o] = piece.astype(BF16)
            dots = dots + piece * xbuf[i, o].astype(F32)
        row = jnp.sum(dots, axis=0, keepdims=True)
        qsend[i] = row
        qbuf[i, me] = row
        rbuf[i, me] = rsend[i, me]
        start((r_copy, q_copy), i)
        arrive((r_copy, q_copy), i)
        w = jnp.zeros((own, br), F32)
        for o in range(n):
            w = w + rbuf[i, o].astype(F32)
        w = w * scale
        overlap = total(jnp.sum(qbuf[i], axis=0)) * scale * scale
        q = overlap / square
        missing = jnp.sum((v - scale * ub.astype(F32)) * w, axis=0, keepdims=True)
        u = v - pre * (w - q * v)
        ub = u.astype(BF16)
        offer(i + 1, u, missing)
        if i + 1 < ITERS:
            offer_x(i + 1, ub)
            start((x_copy, u_copy), i + 1)
        else:
            start((u_copy,), i + 1)
            part[...] = lax.dot_general(
                rot_ref[...], u, (((0,), (0,)), ((), ())),
                precision=lax.Precision.HIGHEST, preferred_element_type=F32)
            parity = lax.rem(me, 2)
            half = part.shape[0] // 2
            give = copy(part.at[pl.ds(pl.multiple_of((1 - parity) * half, half), half)],
                        got, p_out, p_in, me + 1 - 2 * parity)
            give.start()

    give.wait_recv()
    keep = part[pl.ds(pl.multiple_of(parity * half, half), half)]
    out_ref[...] = (keep + got[...]) * scale
    give.wait_send()
    for i in range(ITERS):
        sent((x_copy, u_copy, r_copy, q_copy), i)
    sent((u_copy,), ITERS)


def dense_body(psi_start, precond, left_ops, right_ops, term_in, term_out, term_live, left_rot):
    n = lax.axis_size("ops")
    slots, bl = left_ops.shape[0], left_ops.shape[1]
    own, br = psi_start.shape
    kept = left_rot.shape[1]
    sectors = n * own // bl
    st = sectors * SUB
    vmem = pl.BlockSpec(memory_space=pltpu.VMEM)
    smem = pl.BlockSpec(memory_space=pltpu.SMEM)
    dma = pltpu.SemaphoreType.DMA
    return pl.pallas_call(
        functools.partial(kernel, n),
        out_shape=(
            jax.ShapeDtypeStruct((1,), F32),
            jax.ShapeDtypeStruct((ITERS - 1,), F32),
            jax.ShapeDtypeStruct((kept // 2, br), F32),
        ),
        in_specs=[smem] + [vmem] * 7,
        out_specs=(smem, smem, vmem),
        scratch_shapes=[
            pltpu.VMEM((st, slots * 2 * st), BF16),
            pltpu.VMEM((slots * bl, sectors * br), BF16),
            pltpu.VMEM((slots * 2 * st, bl // SUB * br), BF16),
            pltpu.VMEM((ITERS, own, br), BF16),
            pltpu.VMEM((ITERS, n, own, br), BF16),
            pltpu.VMEM((ITERS, n, own, br), BF16),
            pltpu.VMEM((ITERS, n, own, br), BF16),
            pltpu.VMEM((ITERS, 1, br), F32),
            pltpu.VMEM((ITERS, n, 1, br), F32),
            pltpu.VMEM((ITERS + 1, 2, br), F32),
            pltpu.VMEM((ITERS + 1, n, 2, br), F32),
            pltpu.VMEM((kept, br), F32),
            pltpu.VMEM((kept // 2, br), F32),
            dma((ITERS, n)), dma((ITERS, n)), dma((ITERS, n)), dma((ITERS, n)),
            dma((ITERS, n)), dma((ITERS, n)), dma((ITERS + 1, n)), dma((ITERS + 1, n)),
            dma, dma,
        ],
        compiler_params=pltpu.CompilerParams(
            collective_id=0, has_side_effects=True, vmem_limit_bytes=40 * 2**20),
    )(term_live, psi_start, precond, left_ops, right_ops, term_in, term_out, left_rot)


def body(psi_start, precond, left_ops, right_ops, term_in, term_out, term_live, left_rot):
    n = lax.axis_size("ops")
    own = psi_start.shape[0]
    bl = left_ops.shape[1]
    sectors = n * own // bl
    dense = sectors <= term_in.shape[1] and own % SUB == 0 and bl == 2 * own
    run = dense_body if dense else pair_body
    return run(psi_start, precond, left_ops, right_ops, term_in, term_out, term_live, left_rot)


def solution(mesh):
    rows = P(("groups", "ops"), None)
    blocks = P(("groups", "ops"), None, None)
    return jax.shard_map(
        body,
        mesh=mesh,
        in_specs=(rows, rows, blocks, blocks, rows, rows, P(("groups", "ops")), rows),
        out_specs=(P("groups"), P("groups"), rows),
        check_vma=False,
    )
```

time: 517 us -> 78.1 us (0.15); the launches traced: 509 us -> 77.5 us
  waiting for transfers between devices: 336 us -> 0 us
  matrix products: 73.3 us -> 0 us
  Pallas kernels: 0 us -> 67.9 us
  blocking collectives: 42.4 us -> 0 us
  between operations: 24.2 us -> 2.99 us
  other arithmetic: 15.2 us -> 0 us
  local copies, waits for them, and re-layouts: 16.3 us -> 6.65 us
    psum x4 -> x0, waiting for transfers between devices: 336 us -> none  [body(): image = lax.psum(terms, 'ops')]
    dot_general x9 -> x0, matrix products: 73.3 us -> none  [the longest x4 41.9 us: local_terms(): jnp.dot(onehot.T, flat, precision=lax.Precision.HIGHEST, preferred_elemen...]
    pallas_call x0 -> x1, Pallas kernels: none -> 67.9 us  [dense_body(): pl.pallas_call(functools.partial(kernel, n), out_shape=(jax.ShapeDtypeStr...]
    all_gather x2 -> x0, blocking collectives: 42.4 us -> none  [the longest x1 24 us: body(): lax.all_gather(psi_start, 'ops', axis=0, tiled=True)]
    reduce_sum x8 -> x0, other arithmetic: 13.1 us -> none  [the longest x4 6.6 us: body(): quotient = jnp.sum(vector * image) / jnp.sum(vector * vector)]
    gather x4 -> x0, local copies, waits for them, and re-layouts: 12.3 us -> none  [local_terms(): chosen = blocks[term_in]]
    unnamed x8 -> x16, local copies, waits for them, and re-layouts: 0.02 us -> 6.65 us
  transfers between devices with their start and end apart: 5 -> 0, of which waited for: 5 -> 0; matrix products, arithmetic and copies ran while one was open for 0% -> 0% of each run, Pallas kernels for 0% -> 0%
where the time goes in v1:
time: 78.1 us; the launch traced here: 77.5 us
  Pallas kernels  67.9 us (87%)
  local copies, waits for them, and re-layouts  6.65 us (9%)
  between operations  2.99 us (4%)
    pallas_call x1, Pallas kernels, dense_body(): pl.pallas_call(functools.partial(kernel, n), out_shape=(jax.ShapeDtypeStr...  67.9 us
    unnamed x16, local copies, waits for them, and re-layouts  6.65 us

profile of v1, /device:TPU:0, one launch (start us, length us, event | category | flops | bytes accessed | tf_op | source)
XLA Modules:
  0.0 77.5 jit_solution(14214139258486945416)
XLA Ops:
  1.3 0.0 copy-start
  1.3 1.0 %copy-done = bf16[16,128,128]{2,1,0:T(8,128)(2,1)S(1)} copy-done((bf16[16,128,128]{2,1,0:T(8,128)(2,1)S(1)}, bf16[16,128,128]{2,1,0:T(8,128)(2,1)}, u32[]{:S(2)}) %copy-start) | copy-done | bytes 524312
  2.3 0.0 copy-start.1
  2.3 0.9 %copy-done.1 = bf16[16,64,64]{2,1,0:T(8,128)(2,1)S(1)} copy-done((bf16[16,64,64]{2,1,0:T(8,128)(2,1)S(1)}, bf16[16,64,64]{2,1,0:T(8,128)(2,1)}, u32[]{:S(2)}) %copy-start.1) | copy-done | bytes 131096
  3.3 0.0 copy-start.2
  3.3 0.7 copy-done.2
  4.0 0.0 copy-start.3
  4.0 0.7 copy-done.3
  4.7 0.0 copy-start.4
  4.7 0.7 copy-done.4
  5.4 0.0 copy-start.5
  5.4 0.7 copy-done.5
  6.1 0.0 copy-start.6
  6.1 0.7 copy-done.6
  6.8 67.9 %shard_map.103 = (f32[1]{0:T(128)}, f32[3]{0:T(128)S(1)}, f32[32,128]{1,0:T(8,128)S(1)}) custom-call(s32[1]{0:T(128)S(6)} %copy.14.live_ref, f32[32,128]{1,0:T(8,128)S(1)} %copy-done.2, f32[32,128]{1,0:T(8,128)S(1)} %copy-done.3, bf16[16,64,64]{2,1,0:T(8,128)(2,1)S(1)} %copy-done.1, bf16[16,128,128]{2,1,0:T(8,128)(2,1)S(1)} %copy-done, ...), custom_call_target="tpu_custom_call" | custom-call | tf_op jit(solution)/shard_map/pallas_call | solution.py:299
  75.3 0.5 copy.16
  75.8 0.6 copy.17
Async XLA Ops:
  1.3 1.0 %copy-start = (bf16[16,128,128]{2,1,0:T(8,128)(2,1)S(1)}, bf16[16,128,128]{2,1,0:T(8,128)(2,1)}, u32[]{:S(2)}) copy-start(bf16[16,128,128]{2,1,0:T(8,128)(2,1)} %right_ref.1) | copy-start | bytes 1572868
  2.3 0.9 %copy-start.1 = (bf16[16,64,64]{2,1,0:T(8,128)(2,1)S(1)}, bf16[16,64,64]{2,1,0:T(8,128)(2,1)}, u32[]{:S(2)}) copy-start(bf16[16,64,64]{2,1,0:T(8,128)(2,1)} %left_ref.1) | copy-start | bytes 393220
  3.3 0.7 copy-start.2
  4.0 0.7 copy-start.3
  4.7 0.7 copy-start.4
  5.4 0.7 copy-start.5
  6.1 0.7 copy-start.6

commit v2 on v1

--- a/solution.py
+++ b/solution.py
@@ -82,8 +82,9 @@
 
 def kernel(
     n,
-    live_ref, psi_ref, pre_ref, left_ref, right_ref, tin_ref, tout_ref, rot_ref,
+    live_ref, psi_hbm, tin_hbm, tout_hbm, left_hbm, right_hbm, pre_hbm, rot_hbm,
     first_ref, later_ref, out_ref,
+    psi_ref, tin_ref, tout_ref, left_ref, right_ref, pre_ref, rot_ref, load,
     counts, inner, image, xsend, xbuf, rsend, rbuf, qsend, qbuf, usend, ubuf, part, got,
     x_out, x_in, r_out, r_in, q_out, q_in, u_out, u_in, p_out, p_in,
 ):
@@ -105,6 +106,14 @@
                             device_id_type=pl.DeviceIdType.MESH)
         return carry
 
+    loads = [
+        pltpu.make_async_copy(src, dst, load.at[k])
+        for k, (src, dst) in enumerate((
+            (psi_hbm, psi_ref), (tin_hbm, tin_ref), (tout_hbm, tout_ref), (left_hbm, left_ref),
+            (right_hbm, right_ref), (pre_hbm, pre_ref), (rot_hbm, rot_ref)))
+    ]
+    for one_load in loads:
+        one_load.start()
     lax.fori_loop(1, n, greet, 0)
 
     def copy(src, dst, out_sem, in_sem, to):
@@ -203,13 +212,18 @@
                         axis=0)
         return jnp.dot(counts[...], image[...], preferred_element_type=F32)
 
+    loads[0].wait()
     v = psi_ref[...]
     ub = v.astype(BF16)
     offer_x(0, ub)
     offer(0, v, jnp.zeros((1, br), F32))
     pl.semaphore_wait(barrier, n - 1)
     start((x_copy, u_copy), 0)
+    for k in (1, 2):
+        loads[k].wait()
     build_counts()
+    for k in range(3, len(loads)):
+        loads[k].wait()
     pre = pre_ref[...]
     scale = jnp.ones((1, 1), F32)
     u = v
@@ -296,6 +310,7 @@
     vmem = pl.BlockSpec(memory_space=pltpu.VMEM)
     smem = pl.BlockSpec(memory_space=pltpu.SMEM)
     dma = pltpu.SemaphoreType.DMA
+    loaded = (psi_start, term_in, term_out, left_ops, right_ops, precond, left_rot)
     return pl.pallas_call(
         functools.partial(kernel, n),
         out_shape=(
@@ -303,9 +318,10 @@
             jax.ShapeDtypeStruct((ITERS - 1,), F32),
             jax.ShapeDtypeStruct((kept // 2, br), F32),
         ),
-        in_specs=[smem] + [vmem] * 7,
+        in_specs=[smem] + [pl.BlockSpec(memory_space=pl.ANY)] * 7,
         out_specs=(smem, smem, vmem),
-        scratch_shapes=[
+        scratch_shapes=[pltpu.VMEM(a.shape, a.dtype) for a in loaded] + [
+            dma((len(loaded),)),
             pltpu.VMEM((st, slots * 2 * st), BF16),
             pltpu.VMEM((slots * bl, sectors * br), BF16),
             pltpu.VMEM((slots * 2 * st, bl // SUB * br), BF16),
@@ -324,8 +340,8 @@
             dma, dma,
         ],
         compiler_params=pltpu.CompilerParams(
-            collective_id=0, has_side_effects=True, vmem_limit_bytes=40 * 2**20),
-    )(term_live, psi_start, precond, left_ops, right_ops, term_in, term_out, left_rot)
+            collective_id=0, has_side_effects=True, vmem_limit_bytes=60 * 2**20),
+    )(term_live, *loaded)
 
 
 def body(psi_start, precond, left_ops, right_ops, term_in, term_out, term_live, left_rot):

time: 78.1 us -> 73.3 us (0.939)
  local copies, waits for them, and re-layouts: 6.65 us -> 1.84 us
    unnamed x16 -> x4, local copies, waits for them, and re-layouts: 6.65 us -> 1.84 us
where the time goes in v2:
time: 73.3 us; the launch traced here: 73 us
  Pallas kernels  68 us (93%)
  between operations  3.06 us (4%)
  local copies, waits for them, and re-layouts  1.84 us (3%)
    pallas_call x1, Pallas kernels, dense_body(): pl.pallas_call(functools.partial(kernel, n), out_shape=(jax.ShapeDtypeStr...  68 us
    unnamed x4, local copies, waits for them, and re-layouts  1.84 us

profile of v2, /device:TPU:0, one launch (start us, length us, event | category | flops | bytes accessed | tf_op | source)
XLA Modules:
  0.0 73.0 jit_solution(12103102684606964548)
XLA Ops:
  1.3 68.0 %shard_map.103 = (f32[1]{0:T(128)}, f32[3]{0:T(128)}, f32[32,128]{1,0:T(8,128)}) custom-call(s32[1]{0:T(128)S(6)} %copy.14.live_ref, f32[32,128]{1,0:T(8,128)} %psi_hbm.1, s32[16,16]{1,0:T(8,128)} %tin_hbm.1, s32[16,16]{1,0:T(8,128)} %tout_hbm.1, bf16[16,64,64]{2,1,0:T(8,128)(2,1)} %left_hbm.1, bf16[16,128,128]{2,1,0:T(8,128)(2,1)} %right_hbm.1, ...), custom_call_target="tpu_custom_call" | custom-call | tf_op jit(solution)/shard_map/pallas_call | solution.py:314
  69.3 0.0 copy-start
  70.0 0.0 copy-done
  70.0 0.5 copy.16
  70.5 1.3 %copy.17 = f32[32,128]{1,0:T(8,128)} copy(f32[32,128]{1,0:T(8,128)} %get-tuple-element.8) | data formatting | bytes 32768
Async XLA Ops:
  69.3 0.6 copy-start
